TPU v7x, 32 devices: a whole 2x2x4 slice. The times are simulated.
32 devices in a mesh: groups: 2 (over y), seq: 8 (over z, x), tensor: 2 (over core).
Axes of the slice: x: 2, y: 2, z: 4, core: 2. Of those that a mesh axis runs over, the one named last changes fastest.
Arguments:
- queries: bfloat16 [4096, 2048], P(('groups', 'seq', 'tensor')), parts along dimension 0, may hold values from -80 to 80
- keys: bfloat16 [4096, 1024], P(('groups', 'seq', 'tensor')), parts along dimension 0, may hold values from -4 to 4
- values: bfloat16 [4096, 1024], P(('groups', 'seq', 'tensor')), parts along dimension 0, may hold values from -6 to 6
- block_lists: int32 [16, 32, 12], P(('seq', 'tensor')), may hold values from 0 to 31, as said below
Outputs:
- attended: bfloat16 [4096, 2048], P(('groups', 'seq', 'tensor')), parts along dimension 0
There are 2 independent parts, one for each index of `groups`. A program takes and returns all parts, laid end to end along the dimension named above; an argument that names none is the same for every part. Nothing has to cross between parts.
Inputs may be any that keep to these rules, and one draw needn't show every extreme that they name: `block_lists`: for head h and query block b, slot 0 is b; slots 0 to min(b + 1, 12) - 1 hold distinct blocks at most b; later slots equal b.
All inputs are finite; a program needn't handle non-finite values.
Results may differ from a plain program's by a relative error of at most 0.0041.
Values may be sent and summed in bfloat16 or wider, within the bound.
A program may use at most 128 MiB of HBM per device.

v0:
```python
import jax
import jax.numpy as jnp
from jax import lax
from jax.sharding import PartitionSpec as P

HD = 128
BLK = 64
KSEL = 12
QG = 16


def attend_group(qblk, kfull, vfull, lists, first):
    kblk = kfull[lists]
    vblk = vfull[lists]
    scores = jnp.einsum(
        "gid,gsjd->gisj", qblk, kblk, preferred_element_type=jnp.float32
    ) / jnp.sqrt(jnp.float32(HD))
    qidx = first + jnp.arange(lists.shape[0], dtype=jnp.int32)
    qpos = qidx[:, None] * BLK + jnp.arange(BLK, dtype=jnp.int32)[None, :]
    kpos = lists[:, :, None] * BLK + jnp.arange(BLK, dtype=jnp.int32)[None, None, :]
    slot_live = jnp.arange(KSEL, dtype=jnp.int32)[None, :] < jnp.minimum(qidx + 1, KSEL)[:, None]
    valid = (kpos[:, None, :, :] <= qpos[:, :, None, None]) & slot_live[:, None, :, None]
    masked = jnp.where(valid, scores, jnp.float32(-1e30))
    top = jnp.max(masked, axis=(2, 3), keepdims=True)
    probs = jnp.where(valid, jnp.exp(masked - top), jnp.float32(0.0))
    total = jnp.sum(probs, axis=(2, 3))
    weights = probs.astype(jnp.bfloat16)
    summed = jnp.einsum("gisj,gsjd->gid", weights, vblk, preferred_element_type=jnp.float32)
    return (summed / total[:, :, None]).astype(jnp.bfloat16)


def body(queries, keys, values, block_lists):
    rows = queries.shape[0]
    heads = queries.shape[1] // HD
    kv_heads = keys.shape[1] // HD
    ratio = heads // kv_heads
    n_seq = lax.axis_size("seq")
    n_ten = lax.axis_size("tensor")
    q_three = queries.reshape(rows, heads, HD)
    k_three = jnp.repeat(keys.reshape(rows, kv_heads, HD), ratio, axis=1)
    v_three = jnp.repeat(values.reshape(rows, kv_heads, HD), ratio, axis=1)
    q_head, k_head, v_head = (
        lax.all_to_all(q_three, ("seq", "tensor"), split_axis=1, concat_axis=0, tiled=True),
        lax.all_to_all(k_three, ("seq", "tensor"), split_axis=1, concat_axis=0, tiled=True),
        lax.all_to_all(v_three, ("seq", "tensor"), split_axis=1, concat_axis=0, tiled=True),
    )
    whole = rows * n_seq * n_ten
    blocks = whole // BLK
    kfull = k_head.reshape(blocks, BLK, HD)
    vfull = v_head.reshape(blocks, BLK, HD)
    groups = blocks // QG
    q_groups = q_head.reshape(groups, QG, BLK, HD)
    l_groups = block_lists[0].reshape(groups, QG, KSEL)
    firsts = jnp.arange(groups, dtype=jnp.int32) * QG
    result = lax.map(
        lambda item: attend_group(item[0], kfull, vfull, item[1], item[2]),
        (q_groups, l_groups, firsts),
    )
    back = lax.all_to_all(
        result.reshape(whole, 1, HD), ("seq", "tensor"), split_axis=0, concat_axis=1, tiled=True
    )
    return back.reshape(rows, heads * HD)


def solution(mesh):
    placed = (
        P(("groups", "seq", "tensor"), None),
        P(("groups", "seq", "tensor"), None),
        P(("groups", "seq", "tensor"), None),
        P(("seq", "tensor"), None, None),
    )
    return jax.shard_map(
        body,
        mesh=mesh,
        in_specs=placed,
        out_specs=P(("groups", "seq", "tensor"), None),
        check_vma=False,
    )
```

profile of v0, /device:TPU:0, one launch (start us, length us, event | category | flops | bytes accessed | tf_op | source)
XLA Modules:
  0.0 136.9 jit_solution(3296505927218677360)
XLA Ops:
  0.0 0.0 copy-start
  0.0 0.0 copy-start.2
  0.0 1.1 copy_bitcast_fusion.2
  1.1 0.9 broadcast_in_dim.36
  2.0 7.4 %all-to-all-start.1 = ((bf16[128,16,128]{2,0,1:T(8,128)(2,1)}), bf16[128,16,128]{2,0,1:T(8,128)(2,1)S(1)}, u32[]{:S(2)}, u32[]{:S(2)}) async-start(bf16[128,16,128]{2,0,1:T(8,128)(2,1)} %bitcast.15), calls=%async_computation.1 | async-start | bytes 1048576 | tf_op jit(solution)/shard_map/all_to_all | solution.py:44
  9.3 1.0 copy_bitcast_fusion.1
  10.3 13.5 %all-to-all-done.1 = bf16[128,16,128]{2,0,1:T(8,128)(2,1)S(1)} async-done(((bf16[128,16,128]{2,0,1:T(8,128)(2,1)}), bf16[128,16,128]{2,0,1:T(8,128)(2,1)S(1)}, u32[]{:S(2)}, u32[]{:S(2)}) %all-to-all-start.1) | async-done | bytes 524320 | tf_op jit(solution)/shard_map/all_to_all | solution.py:44
  23.8 0.9 broadcast_in_dim.37
  24.7 4.1 %all-to-all-start.2 = ((bf16[128,16,128]{2,0,1:T(8,128)(2,1)}), bf16[128,16,128]{2,0,1:T(8,128)(2,1)S(1)}, u32[]{:S(2)}, u32[]{:S(2)}) async-start(bf16[128,16,128]{2,0,1:T(8,128)(2,1)} %bitcast.19), calls=%async_computation.2 | async-start | bytes 1048576 | tf_op jit(solution)/shard_map/all_to_all | solution.py:45
  28.8 0.0 copy-done
  28.8 0.9 copy_bitcast_fusion
  29.7 13.5 %all-to-all-done.2 = bf16[128,16,128]{2,0,1:T(8,128)(2,1)S(1)} async-done(((bf16[128,16,128]{2,0,1:T(8,128)(2,1)}), bf16[128,16,128]{2,0,1:T(8,128)(2,1)S(1)}, u32[]{:S(2)}, u32[]{:S(2)}) %all-to-all-start.2) | async-done | bytes 524320 | tf_op jit(solution)/shard_map/all_to_all | solution.py:45
  43.3 4.1 %all-to-all-start = ((bf16[128,16,128]{2,0,1:T(8,128)(2,1)}), bf16[128,16,128]{2,0,1:T(8,128)(2,1)S(1)}, u32[]{:S(2)}, u32[]{:S(2)}) async-start(bf16[128,16,128]{2,0,1:T(8,128)(2,1)} %copy_bitcast_fusion), calls=%async_computation | async-start | bytes 1048576 | tf_op jit(solution)/shard_map/all_to_all | solution.py:43
  47.4 0.0 copy-done.2
  47.4 0.1 copy.30
  47.5 14.4 %all-to-all-done = bf16[128,16,128]{2,0,1:T(8,128)(2,1)S(1)} async-done(((bf16[128,16,128]{2,0,1:T(8,128)(2,1)}), bf16[128,16,128]{2,0,1:T(8,128)(2,1)S(1)}, u32[]{:S(2)}, u32[]{:S(2)}) %all-to-all-start) | async-done | bytes 524320 | tf_op jit(solution)/shard_map/all_to_all | solution.py:43
  61.8 53.1 %while.10 = (s32[]{:T(128)}, bf16[2,16,64,128]{3,2,1,0:T(8,128)(2,1)S(1)}, s32[2,16,12]{2,1,0:T(8,128)S(1)}, s32[2]{0:T(128)S(1)}, bf16[2,16,64,128]{3,2,1,0:T(8...) while((s32[]{:T(128)}, ...), condition=%wide.region_3.4_spmd, body=%wide.region_0.3_spmd.sunk | while | flops 417870848 | bytes 41849104 | solution.py:55
  61.8 0.1 reshape.168
  61.9 2.7 %gather_fusion.1 = bf16[192,64,128]{2,1,0:T(8,128)(2,1)} fusion(bf16[32,64,128]{2,1,0:T(8,128)(2,1)S(1)} %get-tuple-element.133, s32[1024]{0:T(1024)S(1)} %pad_clamp_fusion.2), kind=kCustom, calls=%fused_computation.clone.1 | custom fusion | bytes 6292224 | tf_op jit(solution)/shard_map/while/body/eval_jaxpr/gather | solution.py:13
  64.6 0.1 iota_add_fusion.6
  64.8 0.6 dynamic_slice.27
  65.3 0.6 add_minimum_fusion.2
  66.0 0.1 iota_add_fusion.5
  66.1 0.1 iota_compare_fusion.2
  66.1 6.0 %fusion.41 = (f32[16,64]{1,0:T(8,128)S(1)}, f32[16,64,12,64]{1,3,2,0:T(8,128)S(1)}) fusion(s32[16,64]{1,0:T(8,128)S(1)} %iota_add_fusion.5, s32[16,12,64]{2,1,0:T(8,128)S(1)} %iota_add_fusion.6, pred[16,12]{1,0:T(8,128)(4,1)S(1)} %iota_compare_fusion.2, bf16[16,12,64,128]{3,2,1,0:T(8,128)(2,1)} %bitcast.94, ...), kind=kOutput, calls=%fused_computation.5.clone.1 | convolution fusion | flops 205257728 | bytes 6699012 | tf_op jit(solution)/shard_map/while/body/eval_jaxpr/gid,gsjd->gisj/dot_general | solution.py:15
  72.1 0.0 copy-start.1
  72.1 2.6 %copy-done.1 = f32[16,64,12,64]{1,3,2,0:T(8,128)} copy-done((f32[16,64,12,64]{1,3,2,0:T(8,128)}, f32[16,64,12,64]{1,3,2,0:T(8,128)S(1)}, u32[]{:S(2)}) %copy-start.1) | copy-done | bytes 3145752 | tf_op jit(solution)/shard_map/while
  74.8 3.9 %fusion.42 = f32[16,64]{1,0:T(8,128)S(1)} fusion(f32[16,64]{1,0:T(8,128)S(1)} %get-tuple-element.110, f32[16,64,12,64]{1,3,2,0:T(8,128)S(1)} %get-tuple-element.111, pred[16,12]{1,0:T(8,128)(4,1)S(1)} %iota_compare_fusion.2, s32[16,64]{1,0:T(8,128)S(1)} %iota_add_fusion.5, s32[16,12,64]{2,1,0:T(8,128)S(1)} %iota_add_fusion.6), kind=kLoop, calls=%fused_computation.8.clone.1 | loop fusion | flops 5504000 | bytes 3207360 | tf_op jit(solution)/shard_map/while/body/eval_jaxpr/reduce_sum | solution.py:26
  78.7 2.8 %gather_fusion = bf16[192,64,128]{2,1,0:T(8,128)(2,1)} fusion(bf16[32,64,128]{2,1,0:T(8,128)(2,1)S(1)} %get-tuple-element.134, s32[1024]{0:T(1024)S(1)} %pad_clamp_fusion.2), kind=kCustom, calls=%fused_computation.1.clone.1 | custom fusion | bytes 6292224 | tf_op jit(solution)/shard_map/while/body/eval_jaxpr/gather | solution.py:14
  81.4 6.9 %fusion.43 = bf16[2,16,64,128]{3,2,1,0:T(8,128)(2,1)S(1)} fusion(bf16[2,16,64,128]{3,2,1,0:T(8,128)(2,1)S(1)} %get-tuple-element.121, s32[]{:T(128)} %get-tuple-element.120, bf16[16,12,64,128]{3,2,1,0:T(8,128)(2,1)} %bitcast.95, f32[16,64]{1,0:T(8,128)S(1)} %get-tuple-element.110, f32[16,64,12,64]{1,3,2,0:T(8,128)} %copy-done.1, ...), kind=kOutput, calls=%fused_computation.13.clone.1 | convolution fusion | flops 207093760 | bytes 6711300 | tf_op jit(solution)/shard_map/while/body/eval_jaxpr/gisj,gsjd->gid/dot_general | solution.py:28
  88.4 0.1 reshape.168
  88.5 2.7 %gather_fusion.1 = bf16[192,64,128]{2,1,0:T(8,128)(2,1)} fusion(bf16[32,64,128]{2,1,0:T(8,128)(2,1)S(1)} %get-tuple-element.133, s32[1024]{0:T(1024)S(1)} %pad_clamp_fusion.2), kind=kCustom, calls=%fused_computation.clone.1 | custom fusion | bytes 6292224 | tf_op jit(solution)/shard_map/while/body/eval_jaxpr/gather | solution.py:13
  91.2 0.1 iota_add_fusion.6
  91.3 0.6 dynamic_slice.27
  91.9 0.6 add_minimum_fusion.2
  92.6 0.1 iota_add_fusion.5
  92.6 0.1 iota_compare_fusion.2
  92.7 6.0 %fusion.41 = (f32[16,64]{1,0:T(8,128)S(1)}, f32[16,64,12,64]{1,3,2,0:T(8,128)S(1)}) fusion(s32[16,64]{1,0:T(8,128)S(1)} %iota_add_fusion.5, s32[16,12,64]{2,1,0:T(8,128)S(1)} %iota_add_fusion.6, pred[16,12]{1,0:T(8,128)(4,1)S(1)} %iota_compare_fusion.2, bf16[16,12,64,128]{3,2,1,0:T(8,128)(2,1)} %bitcast.94, ...), kind=kOutput, calls=%fused_computation.5.clone.1 | convolution fusion | flops 205257728 | bytes 6699012 | tf_op jit(solution)/shard_map/while/body/eval_jaxpr/gid,gsjd->gisj/dot_general | solution.py:15
  98.7 0.0 copy-start.1
  98.7 2.6 %copy-done.1 = f32[16,64,12,64]{1,3,2,0:T(8,128)} copy-done((f32[16,64,12,64]{1,3,2,0:T(8,128)}, f32[16,64,12,64]{1,3,2,0:T(8,128)S(1)}, u32[]{:S(2)}) %copy-start.1) | copy-done | bytes 3145752 | tf_op jit(solution)/shard_map/while
  101.3 3.9 %fusion.42 = f32[16,64]{1,0:T(8,128)S(1)} fusion(f32[16,64]{1,0:T(8,128)S(1)} %get-tuple-element.110, f32[16,64,12,64]{1,3,2,0:T(8,128)S(1)} %get-tuple-element.111, pred[16,12]{1,0:T(8,128)(4,1)S(1)} %iota_compare_fusion.2, s32[16,64]{1,0:T(8,128)S(1)} %iota_add_fusion.5, s32[16,12,64]{2,1,0:T(8,128)S(1)} %iota_add_fusion.6), kind=kLoop, calls=%fused_computation.8.clone.1 | loop fusion | flops 5504000 | bytes 3207360 | tf_op jit(solution)/shard_map/while/body/eval_jaxpr/reduce_sum | solution.py:26
  105.3 2.8 %gather_fusion = bf16[192,64,128]{2,1,0:T(8,128)(2,1)} fusion(bf16[32,64,128]{2,1,0:T(8,128)(2,1)S(1)} %get-tuple-element.134, s32[1024]{0:T(1024)S(1)} %pad_clamp_fusion.2), kind=kCustom, calls=%fused_computation.1.clone.1 | custom fusion | bytes 6292224 | tf_op jit(solution)/shard_map/while/body/eval_jaxpr/gather | solution.py:14
  108.0 6.9 %fusion.43 = bf16[2,16,64,128]{3,2,1,0:T(8,128)(2,1)S(1)} fusion(bf16[2,16,64,128]{3,2,1,0:T(8,128)(2,1)S(1)} %get-tuple-element.121, s32[]{:T(128)} %get-tuple-element.120, bf16[16,12,64,128]{3,2,1,0:T(8,128)(2,1)} %bitcast.95, f32[16,64]{1,0:T(8,128)S(1)} %get-tuple-element.110, f32[16,64,12,64]{1,3,2,0:T(8,128)} %copy-done.1, ...), kind=kOutput, calls=%fused_computation.13.clone.1 | convolution fusion | flops 207093760 | bytes 6711300 | tf_op jit(solution)/shard_map/while/body/eval_jaxpr/gisj,gsjd->gid/dot_general | solution.py:28
  115.0 0.5 broadcast.131
  115.5 1.0 reduce
  116.5 0.1 reshape.157
  116.6 18.4 %all_to_all.60 = bf16[16,2,8192]{2,1,0:T(2,128)(2,1)S(1)} all-to-all(bf16[16,2,8192]{2,1,0:T(2,128)(2,1)S(1)} %reshape.157), channel_id=1, replica_groups=mesh['groups'=2,'seq'=8,'tensor'=2] {'seq','tensor'}, dimensions={0} | all-to-all | bytes 1048576 | tf_op jit(solution)/shard_map/all_to_all | solution.py:59
  135.0 0.5 reshape.158
  135.5 0.1 copy.40
  135.6 0.3 copy.35
  135.9 1.0 copy.36
  (8 shorter events, 0.0 us)
Async XLA Ops:
  0.0 28.8 %copy-start = (bf16[128,2048]{1,0:T(8,128)(2,1)S(1)}, bf16[128,2048]{1,0:T(8,128)(2,1)}, u32[]{:S(2)}) copy-start(bf16[128,2048]{1,0:T(8,128)(2,1)} %param.6) | copy-start | bytes 1572868
  0.0 47.4 %copy-start.2 = (s32[1,32,12]{1,0,2:T(1,128)S(1)}, s32[1,32,12]{1,0,2:T(1,128)}, u32[]{:S(2)}) copy-start(s32[1,32,12]{1,0,2:T(1,128)} %param.9) | copy-start | bytes 4612
  2.0 21.8 %all-to-all-start.1 = ((bf16[128,16,128]{2,0,1:T(8,128)(2,1)}), bf16[128,16,128]{2,0,1:T(8,128)(2,1)S(1)}, u32[]{:S(2)}, u32[]{:S(2)}) async-start(bf16[128,16,128]{2,0,1:T(8,128)(2,1)} %bitcast.15), calls=%async_computation.1 | async-start | bytes 1048576 | tf_op jit(solution)/shard_map/all_to_all | solution.py:44
  24.7 18.6 %all-to-all-start.2 = ((bf16[128,16,128]{2,0,1:T(8,128)(2,1)}), bf16[128,16,128]{2,0,1:T(8,128)(2,1)S(1)}, u32[]{:S(2)}, u32[]{:S(2)}) async-start(bf16[128,16,128]{2,0,1:T(8,128)(2,1)} %bitcast.19), calls=%async_computation.2 | async-start | bytes 1048576 | tf_op jit(solution)/shard_map/all_to_all | solution.py:45
  43.3 18.6 %all-to-all-start = ((bf16[128,16,128]{2,0,1:T(8,128)(2,1)}), bf16[128,16,128]{2,0,1:T(8,128)(2,1)S(1)}, u32[]{:S(2)}, u32[]{:S(2)}) async-start(bf16[128,16,128]{2,0,1:T(8,128)(2,1)} %copy_bitcast_fusion), calls=%async_computation | async-start | bytes 1048576 | tf_op jit(solution)/shard_map/all_to_all | solution.py:43
  72.1 2.6 %copy-start.1 = (f32[16,64,12,64]{1,3,2,0:T(8,128)}, f32[16,64,12,64]{1,3,2,0:T(8,128)S(1)}, u32[]{:S(2)}) copy-start(f32[16,64,12,64]{1,3,2,0:T(8,128)S(1)} %get-tuple-element.111) | copy-start | bytes 9437188 | tf_op jit(solution)/shard_map/while
  98.7 2.6 %copy-start.1 = (f32[16,64,12,64]{1,3,2,0:T(8,128)}, f32[16,64,12,64]{1,3,2,0:T(8,128)S(1)}, u32[]{:S(2)}) copy-start(f32[16,64,12,64]{1,3,2,0:T(8,128)S(1)} %get-tuple-element.111) | copy-start | bytes 9437188 | tf_op jit(solution)/shard_map/while
where the time goes:
time: 138 us; the launch traced here: 137 us
  waiting for transfers between devices  41.3 us (30%)
  matrix products  25.8 us (19%)
  local copies, waits for them, and re-layouts  24.9 us (18%)
  blocking collectives  18.4 us (13%)
  starting transfers between devices  15.6 us (11%)
  other arithmetic  10.7 us (8%)
    all_to_all x1, blocking collectives, body(): lax.all_to_all(result.reshape(whole, 1, HD), ('seq', 'tensor'), split_axi...  18.4 us
    all_to_all x1, waiting for transfers between devices, body(): lax.all_to_all(q_three, ('seq', 'tensor'), split_axis=1, concat_axis=0, t...  14.4 us
    dot_general x2, matrix products, attend_group(): jnp.einsum('gisj,gsjd->gid', weights, vblk, preferred_element_type=jnp.fl...  13.8 us
    all_to_all x1, waiting for transfers between devices, body(): lax.all_to_all(v_three, ('seq', 'tensor'), split_axis=1, concat_axis=0, t...  13.5 us
    all_to_all x1, waiting for transfers between devices, body(): lax.all_to_all(k_three, ('seq', 'tensor'), split_axis=1, concat_axis=0, t...  13.5 us
    dot_general x2, matrix products, attend_group(): jnp.einsum('gid,gsjd->gisj', qblk, kblk, preferred_element_type=jnp.float32)  11.9 us
    reduce_sum x2, other arithmetic, attend_group(): total = jnp.sum(probs, axis=(2, 3))  7.85 us
    all_to_all x1, starting transfers between devices, body(): lax.all_to_all(k_three, ('seq', 'tensor'), split_axis=1, concat_axis=0, t...  7.36 us
  transfers between devices with their start and end apart: 3, of which 3 were waited for; matrix products, arithmetic and copies ran while one was open for 1% of the time, Pallas kernels for 0%

commit v1 on v0

v1 whole, which is shorter than its diff:
```python
import functools

import jax
import jax.numpy as jnp
from jax import lax
from jax.experimental import pallas as pl
from jax.experimental.pallas import tpu as pltpu
from jax.sharding import PartitionSpec as P

HD = 128
BLK = 64
KSEL = 12
MESH = pl.DeviceIdType.MESH
COEF = 1.4426950408889634 / (128.0**0.5)


def attend_block(qblk, kcat, vcat, block):
    raw = lax.dot_general(qblk, kcat, (((1,), (1,)), ((), ())), preferred_element_type=jnp.float32)
    row = lax.broadcasted_iota(jnp.int32, raw.shape, 0)
    col = lax.broadcasted_iota(jnp.int32, raw.shape, 1)
    live = jnp.minimum(block + 1, KSEL) * BLK
    keep = ((col >= BLK) | (col <= row)) & (col < live)
    raw = jnp.where(keep, raw, jnp.float32(-1e30))
    top = jnp.max(raw, axis=1, keepdims=True)
    probs = jnp.exp2((raw - top) * jnp.float32(COEF))
    total = jnp.sum(probs, axis=1, keepdims=True)
    summed = jnp.dot(probs.astype(jnp.bfloat16), vcat, preferred_element_type=jnp.float32)
    return (summed / total).astype(jnp.bfloat16)


def kernel(nc, nt, ratio, mult, lists, q, k, v, out, qh, kv, oh,
           s_kv, s_q, s_o, s_f, s_s, l_kv, l_o, r_kv, r_f, r_s, r_q, r_o):
    n = nc * nt
    rows = q.shape[0]
    per = rows // BLK
    c, t = lax.axis_index("seq"), lax.axis_index("tensor")
    me = c * nt + t
    sib = 1 - t

    def dev(chip, core):
        return {"seq": chip, "tensor": core}

    def part(index):
        return pl.ds(pl.multiple_of(index * rows, rows), rows)

    def blocks(index):
        return pl.ds(index * per, per)

    def cols(head):
        return pl.ds(pl.multiple_of(head * HD, HD), HD)

    def remote(src, dst, send, recv, chip, core):
        return pltpu.make_async_remote_copy(
            src_ref=src, dst_ref=dst, send_sem=send, recv_sem=recv,
            device_id=dev(chip, core), device_id_type=MESH,
        )

    def drain(ref, sem):
        pltpu.make_async_copy(ref, ref, sem).wait()

    def loop(start, stop, step):
        def run(i, _):
            step(i)
            return 0
        lax.fori_loop(start, stop, run, 0)

    barrier = pltpu.get_barrier_semaphore()

    def greet(i):
        p = lax.rem(me + i, n)
        pl.semaphore_signal(barrier, inc=1, device_id=dev(p // nt, lax.rem(p, nt)), device_id_type=MESH)

    loop(1, n, greet)
    pl.semaphore_wait(barrier, n - 1)

    def send_kv(j):
        dc = lax.rem(c + j * mult, nc)
        head = cols((dc * nt) // ratio)
        for core, src in ((0, k), (1, v)):
            remote(src.at[:, :, head], kv.at[core, blocks(me)], s_kv, r_kv.at[me], dc, core).start()

    loop(1, nc, send_kv)
    head = cols(me // ratio)
    local = []
    for core, src in ((0, k), (1, v)):
        remote(src.at[:, :, head], kv.at[core, blocks(me)], s_s.at[core], r_s.at[core], c, sib).start()
        local.append(pltpu.make_async_copy(src.at[:, :, head], kv.at[core, blocks(me)], l_kv.at[core]))
        local[-1].start()

    pltpu.make_async_copy(q.at[:, cols(me)], qh.at[part(me)], r_q.at[me]).start()
    remote(q.at[:, cols(c * nt + sib)], qh.at[part(me)], s_q, r_q.at[me], c, sib).start()

    def send_q(j):
        dc = lax.rem(c + j * mult, nc)
        for core in range(nt):
            remote(q.at[:, cols(dc * nt + core)], qh.at[part(me)], s_q, r_q.at[me], dc, core).start()

    loop(1, nc, send_q)

    def forward(j):
        sc = lax.rem(c + (nc - j) * mult, nc)
        for core in range(nt):
            s = sc * nt + core
            drain(kv.at[t, blocks(s)], r_kv.at[s])
            remote(kv.at[t, blocks(s)], kv.at[t, blocks(s)], s_f, r_f, c, sib).start()

    loop(1, nc, forward)
    for core in range(nt):
        local[core].wait()
        drain(kv.at[core, blocks(0)], r_s.at[core])
    drain(kv.at[0, pl.ds(0, (n - nt) * per)], r_f)

    def attend(i):
        j = i // nt
        sc = lax.rem(c + (nc - j) * mult, nc)
        score = lax.rem(t + i, nt)
        s = sc * nt + score
        drain(qh.at[part(s)], r_q.at[s])
        for inner in range(per):
            block = s * per + inner
            listed = [lists[block * KSEL + slot] for slot in range(KSEL)]
            kcat = jnp.concatenate([kv[0, i] for i in listed], axis=0)
            vcat = jnp.concatenate([kv[1, i] for i in listed], axis=0)
            here = pl.ds(pl.multiple_of(block * BLK, BLK), BLK)
            oh[here, :] = attend_block(qh[here, :], kcat, vcat, block)

        @pl.when(i == 0)
        def _():
            pltpu.make_async_copy(oh.at[part(s)], out.at[:, cols(me)], l_o).start()

        @pl.when(i > 0)
        def _():
            remote(oh.at[part(s)], out.at[:, cols(me)], s_o, r_o, sc, score).start()

    loop(0, n, attend)

    drain(oh.at[part(0)], l_o)
    others = pl.ds(0, (n - 1) * HD)
    drain(out.at[:, others], r_o)
    drain(out.at[:, others], s_o)
    drain(out.at[:, others], s_q)
    drain(kv.at[0, pl.ds(0, (n - nt) * per)], s_kv)
    drain(kv.at[0, pl.ds(0, (n - nt) * per)], s_f)
    for core in range(nt):
        drain(kv.at[core, blocks(0)], s_s.at[core])


def body(nc, nt, queries, keys, values, block_lists):
    rows, width = queries.shape
    n = nc * nt
    heads = width // HD
    kv_heads = keys.shape[1] // HD
    ratio = heads // kv_heads
    assert nt == 2 and heads == n and ratio % nt == 0 and rows % BLK == 0
    mult = nc // 2 - 1 if nc >= 4 and nc & (nc - 1) == 0 else 1
    dma, shape = pltpu.SemaphoreType.DMA, jax.ShapeDtypeStruct
    hbm = pl.BlockSpec(memory_space=pl.ANY)
    return pl.pallas_call(
        functools.partial(kernel, nc, nt, ratio, mult),
        out_shape=shape((rows, width), jnp.bfloat16),
        in_specs=[pl.BlockSpec(memory_space=pltpu.SMEM), hbm, hbm, hbm],
        out_specs=hbm,
        scratch_shapes=[
            pltpu.VMEM((n * rows, HD), jnp.bfloat16),
            pltpu.VMEM((2, n * rows // BLK, BLK, HD), jnp.bfloat16),
            pltpu.VMEM((n * rows, HD), jnp.bfloat16),
            dma, dma, dma, dma, dma((nt,)), dma((nt,)), dma,
            dma((n,)), dma, dma((nt,)), dma((n,)), dma,
        ],
        compiler_params=pltpu.CompilerParams(
            collective_id=0, has_side_effects=True, vmem_limit_bytes=40 * 2**20
        ),
        cost_estimate=pl.CostEstimate(
            flops=4 * n * rows * KSEL * BLK * HD, bytes_accessed=8 * n * rows * HD, transcendentals=n * rows * KSEL * BLK
        ),
    )(
        block_lists.reshape(-1),
        queries,
        keys.reshape(rows // BLK, BLK, kv_heads * HD),
        values.reshape(rows // BLK, BLK, kv_heads * HD),
    )


def solution(mesh):
    placed = (
        P(("groups", "seq", "tensor"), None),
        P(("groups", "seq", "tensor"), None),
        P(("groups", "seq", "tensor"), None),
        P(("seq", "tensor"), None, None),
    )
    return jax.shard_map(
        functools.partial(body, mesh.shape["seq"], mesh.shape["tensor"]),
        mesh=mesh,
        in_specs=placed,
        out_specs=P(("groups", "seq", "tensor"), None),
        check_vma=False,
    )
```

time: 138 us -> 48.4 us (0.35)
  Pallas kernels: 0 us -> 43.6 us
  waiting for transfers between devices: 41.3 us -> 0 us
  matrix products: 25.8 us -> 0 us
  local copies, waits for them, and re-layouts: 24.9 us -> 4.61 us
  blocking collectives: 18.4 us -> 0 us
  starting transfers between devices: 15.6 us -> 0 us
  other arithmetic: 10.7 us -> 0 us
    pallas_call x0 -> x1, Pallas kernels: none -> 43.6 us  [body(): pl.pallas_call(functools.partial(kernel, nc, nt, ratio, mult), out_shape=...]
    all_to_all x3 -> x0, waiting for transfers between devices: 41.3 us -> none  [the longest x1 14.4 us: body(): lax.all_to_all(q_three, ('seq', 'tensor'), split_axis=1, concat_axis=0, t...]
    dot_general x4 -> x0, matrix products: 25.8 us -> none  [the longest x2 13.8 us: attend_group(): jnp.einsum('gisj,gsjd->gid', weights, vblk, preferred_element_type=jnp.fl...]
    all_to_all x1 -> x0, blocking collectives: 18.4 us -> none  [body(): lax.all_to_all(result.reshape(whole, 1, HD), ('seq', 'tensor'), split_axi...]
    all_to_all x3 -> x0, starting transfers between devices: 15.6 us -> none  [the longest x1 7.36 us: body(): lax.all_to_all(k_three, ('seq', 'tensor'), split_axis=1, concat_axis=0, t...]
    gather x4 -> x0, local copies, waits for them, and re-layouts: 10.9 us -> none  [the longest x2 5.52 us: attend_group(): vblk = vfull[lists]]
    reduce_sum x2 -> x0, other arithmetic: 7.85 us -> none  [attend_group(): total = jnp.sum(probs, axis=(2, 3))]
    while x4 -> x0, local copies, waits for them, and re-layouts: 5.27 us -> none
  transfers between devices with their start and end apart: 3 -> 0, of which waited for: 3 -> 0; matrix products, arithmetic and copies ran while one was open for 1% -> 0% of each run, Pallas kernels for 0% -> 0%
where the time goes in v1:
time: 48.4 us; the launch traced here: 48.2 us
  Pallas kernels  43.6 us (90%)
  local copies, waits for them, and re-layouts  4.61 us (10%)
    pallas_call x1, Pallas kernels, body(): pl.pallas_call(functools.partial(kernel, nc, nt, ratio, mult), out_shape=...  43.6 us
    unnamed x8, local copies, waits for them, and re-layouts  4.5 us

profile of v1, /device:TPU:0, one launch (start us, length us, event | category | flops | bytes accessed | tf_op | source)
XLA Modules:
  0.0 48.2 jit_solution(2124823309422815603)
XLA Ops:
  0.0 0.8 %copy.5 = s32[1,32,12]{2,1,0:T(8,128)S(1)} copy(s32[1,32,12]{1,0,2:T(1,128)} %param.7) | data formatting | bytes 3072 | tf_op args[3]
  0.8 0.1 reshape.9.lists
  0.9 0.0 copy-start
  0.9 1.0 %copy-done = bf16[128,2048]{1,0:T(8,128)(2,1)S(1)} copy-done((bf16[128,2048]{1,0:T(8,128)(2,1)S(1)}, bf16[128,2048]{1,0:T(8,128)(2,1)}, u32[]{:S(2)}) %copy-start) | copy-done | bytes 524312
  1.9 0.0 copy-start.1
  1.9 0.9 %copy-done.1 = bf16[128,1024]{1,0:T(8,128)(2,1)S(1)} copy-done((bf16[128,1024]{1,0:T(8,128)(2,1)S(1)}, bf16[128,1024]{1,0:T(8,128)(2,1)}, u32[]{:S(2)}) %copy-start.1) | copy-done | bytes 262168
  2.9 0.0 copy-start.2
  2.9 0.9 %copy-done.2 = bf16[128,1024]{1,0:T(8,128)(2,1)S(1)} copy-done((bf16[128,1024]{1,0:T(8,128)(2,1)S(1)}, bf16[128,1024]{1,0:T(8,128)(2,1)}, u32[]{:S(2)}) %copy-start.2) | copy-done | bytes 262168
  3.8 43.6 %shard_map.46 = bf16[128,2048]{1,0:T(8,128)(2,1)S(1)} custom-call(s32[384]{0:T(512)S(1)} %reshape.9.lists, bf16[128,2048]{1,0:T(8,128)(2,1)S(1)} %copy-done, bf16[2,64,1024]{2,1,0:T(8,128)(2,1)S(1)} %bitcast.2, bf16[2,64,1024]{2,1,0:T(8,128)(2,1)S(1)} %bitcast.3), custom_call_target="tpu_custom_call" | custom-call | flops 805306368 | bytes 2097152 | tf_op jit(solution)/shard_map/pallas_call | solution.py:158
  47.4 0.8 %copy.7 = bf16[128,2048]{1,0:T(8,128)(2,1)} copy(bf16[128,2048]{1,0:T(8,128)(2,1)S(1)} %shard_map.46) | data formatting | bytes 1048576
Async XLA Ops:
  0.9 1.0 %copy-start = (bf16[128,2048]{1,0:T(8,128)(2,1)S(1)}, bf16[128,2048]{1,0:T(8,128)(2,1)}, u32[]{:S(2)}) copy-start(bf16[128,2048]{1,0:T(8,128)(2,1)} %q.1) | copy-start | bytes 1572868
  1.9 0.9 %copy-start.1 = (bf16[128,1024]{1,0:T(8,128)(2,1)S(1)}, bf16[128,1024]{1,0:T(8,128)(2,1)}, u32[]{:S(2)}) copy-start(bf16[128,1024]{1,0:T(8,128)(2,1)} %param.5) | copy-start | bytes 786436
  2.9 0.9 %copy-start.2 = (bf16[128,1024]{1,0:T(8,128)(2,1)S(1)}, bf16[128,1024]{1,0:T(8,128)(2,1)}, u32[]{:S(2)}) copy-start(bf16[128,1024]{1,0:T(8,128)(2,1)} %param.6) | copy-start | bytes 786436

commit v2 on v1

--- a/solution.py
+++ b/solution.py
@@ -10,6 +10,7 @@
 HD = 128
 BLK = 64
 KSEL = 12
+VMEM_MIB = 60
 MESH = pl.DeviceIdType.MESH
 COEF = 1.4426950408889634 / (128.0**0.5)
 
@@ -145,6 +146,260 @@
         drain(kv.at[core, blocks(0)], s_s.at[core])
 
 
+def halves_kernel(nc, lists, q, k, v, out, lv, ls, qh, kva, kvb, oh,
+                  s_l, r_l, c_l, s_own, s_up, s_q, s_o, s_f, s_s, l_kv, r_kv, r_f, r_s, r_q, r_o):
+    nt = 2
+    n = nc * nt
+    half = nc // 2
+    row = half // 2
+    rows = q.shape[0]
+    per = rows // BLK
+    kvs = (kva, kvb)
+    c, t = lax.axis_index("seq"), lax.axis_index("tensor")
+    me = c * nt + t
+    sib = 1 - t
+    hz, cx = c // half, lax.rem(c, half)
+    base = hz * half
+    tz = cx // row
+    mine = lax.rem(cx, row) * nt + t
+
+    def dev(chip, core):
+        return {"seq": chip, "tensor": core}
+
+    def blocks(index):
+        return pl.ds(index * per, per)
+
+    def cols(index, width):
+        return pl.ds(pl.multiple_of(index * width, width), width)
+
+    def remote(src, dst, send, recv, chip, core):
+        return pltpu.make_async_remote_copy(
+            src_ref=src, dst_ref=dst, send_sem=send, recv_sem=recv,
+            device_id=dev(chip, core), device_id_type=MESH,
+        )
+
+    def drain(ref, sem):
+        pltpu.make_async_copy(ref, ref, sem).wait()
+
+    def loop(start, stop, step):
+        def run(i, _):
+            step(i)
+            return 0
+        lax.fori_loop(start, stop, run, 0)
+
+    barrier = pltpu.get_barrier_semaphore()
+
+    def greet(i):
+        p = lax.rem(me + i, n)
+        pl.semaphore_signal(barrier, inc=1, device_id=dev(p // nt, lax.rem(p, nt)), device_id_type=MESH)
+
+    loop(1, n, greet)
+    pl.semaphore_wait(barrier, n - 1)
+
+    def send_kv(j, dc, sem):
+        at = cols((lax.rem(dc, half)) * 2 + j, HD)
+        for core, src in ((0, k), (1, v)):
+            remote(src.at[:, :, at], kvs[j].at[core, blocks(me)], sem, r_kv.at[j, me], dc, core).start()
+
+    def send_up(j):
+        @pl.when(hz == 0)
+        def _():
+            loop(0, half, lambda i: send_kv(j, half + lax.rem(cx + i, half), s_up))
+
+    def send_own(j):
+        loop(1, half, lambda i: send_kv(j, base + lax.rem(cx + i, half), s_own))
+        at = cols(cx * 2 + j, HD)
+        for core, src in ((0, k), (1, v)):
+            remote(src.at[:, :, at], kvs[j].at[core, blocks(me)], s_s.at[j, core], r_s.at[j, core], c, sib).start()
+            pltpu.make_async_copy(src.at[:, :, at], kvs[j].at[core, blocks(me)], l_kv.at[j, core]).start()
+
+    send_up(0)
+
+    entry = lax.rem(me, 4)
+    for far in range(2):
+        dc = far * half + me // 4
+        for core in range(nt):
+            itself = (dc == c) & (t == core)
+
+            @pl.when(itself)
+            def _():
+                pltpu.make_async_copy(lists, lv.at[entry], r_l.at[entry]).start()
+
+            @pl.when(jnp.logical_not(itself))
+            def _():
+                remote(lists, lv.at[entry], s_l.at[far, core], r_l.at[entry], dc, core).start()
+
+    send_own(0)
+
+    def send_q(i):
+        cl = lax.rem(cx + i, half)
+        remote(q.at[:, cols(cl, 4 * HD)], qh.at[mine], s_q, r_q.at[mine], base + cl, tz).start()
+
+    @pl.when(tz == t)
+    def _():
+        pltpu.make_async_copy(q.at[:, cols(cx, 4 * HD)], qh.at[mine], r_q.at[mine]).start()
+
+    @pl.when(tz != t)
+    def _():
+        send_q(0)
+
+    loop(1, half, send_q)
+    send_up(1)
+    send_own(1)
+
+    def forward(j, chip):
+        for core in range(nt):
+            here = kvs[j].at[t, blocks(chip * nt + core)]
+            drain(here, r_kv.at[j, chip * nt + core])
+            remote(here, here, s_f.at[j], r_f.at[j], c, sib).start()
+
+    def forward_own(j):
+        loop(1, half, lambda i: forward(j, base + lax.rem(cx + half - i, half)))
+
+    def settle(j):
+        for core in range(nt):
+            drain(kvs[j].at[core, blocks(0)], r_s.at[j, core])
+            drain(kvs[j].at[core, blocks(0)], l_kv.at[j, core])
+
+        @pl.when(hz == 0)
+        def _():
+            drain(kvs[j].at[0, pl.ds(0, (half - 1) * nt * per)], r_f.at[j])
+
+        @pl.when(hz == 1)
+        def _():
+            drain(kvs[j].at[0, pl.ds(0, (nc - 1) * nt * per)], r_f.at[j])
+
+    forward_own(0)
+
+    @pl.when(hz == 1)
+    def _():
+        loop(0, half, lambda i: forward(0, lax.rem(cx + half - i, half)))
+
+    for e in range(4):
+        drain(lv.at[e], r_l.at[e])
+    pltpu.make_async_copy(lv, ls, c_l).start()
+    settle(0)
+    pltpu.make_async_copy(lv, ls, c_l).wait()
+
+    def attend(j, i):
+        slot = lax.rem(mine + i, 4)
+        sc, score = base + t * row + slot // nt, lax.rem(slot, nt)
+        if j == 0:
+            drain(qh.at[slot], r_q.at[slot])
+        for inner in range(per):
+            block = (sc * nt + score) * per + inner
+            here = pl.ds(inner * BLK, BLK)
+            for one in range(2):
+                head = 2 * j + one
+                listed = [ls[head, e, 0, block] for e in range(KSEL)]
+                kcat = jnp.concatenate([kvs[j][0, e] for e in listed], axis=0)
+                vcat = jnp.concatenate([kvs[j][1, e] for e in listed], axis=0)
+                qblk = qh[slot, here, pl.ds(head * HD, HD)]
+                oh[slot, j, here, pl.ds(one * HD, HD)] = attend_block(qblk, kcat, vcat, block)
+        itself = (sc == c) & (score == t)
+        goal = out.at[:, cols(cx * 2 + j, 2 * HD)]
+
+        @pl.when(itself)
+        def _():
+            pltpu.make_async_copy(oh.at[slot, j], goal, r_o.at[cx, j]).start()
+
+        @pl.when(jnp.logical_not(itself))
+        def _():
+            remote(oh.at[slot, j], goal, s_o, r_o.at[cx, j], sc, score).start()
+
+    def first(i):
+        @pl.when(i == 0)
+        def _():
+            forward_own(1)
+
+        attend(0, i)
+
+        @pl.when(hz == 1)
+        def _():
+            forward(1, lax.rem(cx + half - i, half))
+
+    loop(0, 4, first)
+    settle(1)
+    loop(0, 4, lambda i: attend(1, i))
+
+    for cl in range(half):
+        for j in range(2):
+            drain(out.at[:, pl.ds((cl * 2 + j) * 2 * HD, 2 * HD)], r_o.at[cl, j])
+
+    @pl.when(tz == t)
+    def _():
+        drain(out.at[:, pl.ds(0, 3 * 4 * HD)], s_q)
+
+    @pl.when(tz != t)
+    def _():
+        drain(out, s_q)
+
+    @pl.when((base + t * row == c - lax.rem(cx, row)))
+    def _():
+        drain(out.at[:, pl.ds(0, 6 * 2 * HD)], s_o)
+
+    @pl.when((base + t * row != c - lax.rem(cx, row)))
+    def _():
+        drain(out, s_o)
+
+    drain(kva.at[0, pl.ds(0, (half - 1) * 4 * per)], s_own)
+
+    @pl.when(hz == 0)
+    def _():
+        drain(kva.at[0], s_up)
+
+    for j in range(2):
+        @pl.when(hz == 0)
+        def _():
+            drain(kva.at[0, pl.ds(0, (half - 1) * nt * per)], s_f.at[j])
+
+        @pl.when(hz == 1)
+        def _():
+            drain(kva.at[0, pl.ds(0, (nc - 1) * nt * per)], s_f.at[j])
+
+        for core in range(nt):
+            drain(kva.at[core, blocks(0)], s_s.at[j, core])
+
+    for far in range(2):
+        dc = far * half + me // 4
+        for core in range(nt):
+            @pl.when(jnp.logical_not((dc == c) & (t == core)))
+            def _():
+                drain(lv.at[0], s_l.at[far, core])
+
+
+def halves(nc, queries, keys, values, block_lists):
+    rows, width = queries.shape
+    n = 2 * nc
+    per = rows // BLK
+    dma = pltpu.SemaphoreType.DMA
+    hbm = pl.BlockSpec(memory_space=pl.ANY)
+    entry = (KSEL, 1, block_lists.shape[1])
+    kv = pltpu.VMEM((2, n * per, BLK, HD), jnp.bfloat16)
+    return pl.pallas_call(
+        functools.partial(halves_kernel, nc),
+        out_shape=jax.ShapeDtypeStruct((rows, width), jnp.bfloat16),
+        in_specs=[hbm, hbm, hbm, hbm],
+        out_specs=hbm,
+        scratch_shapes=[
+            pltpu.VMEM((4, *entry), jnp.int32),
+            pltpu.SMEM((4, *entry), jnp.int32),
+            pltpu.VMEM((4, rows, 4 * HD), jnp.bfloat16),
+            kv,
+            kv,
+            pltpu.VMEM((4, 2, rows, 2 * HD), jnp.bfloat16),
+            dma((2, 2)), dma((4,)), dma, dma, dma, dma, dma, dma((2,)), dma((2, 2)), dma((2, 2)),
+            dma((2, n)), dma((2,)), dma((2, 2)), dma((4,)), dma((nc // 2, 2)),
+        ],
+        compiler_params=pltpu.CompilerParams(
+            collective_id=0, has_side_effects=True, vmem_limit_bytes=VMEM_MIB * 2**20
+        ),
+        cost_estimate=pl.CostEstimate(
+            flops=4 * n * rows * KSEL * BLK * HD, bytes_accessed=8 * n * rows * HD, transcendentals=n * rows * KSEL * BLK
+        ),
+    )(block_lists.transpose(2, 0, 1), queries, keys.reshape(per, BLK, -1), values.reshape(per, BLK, -1))
+
+
 def body(nc, nt, queries, keys, values, block_lists):
     rows, width = queries.shape
     n = nc * nt
@@ -152,6 +407,8 @@
     kv_heads = keys.shape[1] // HD
     ratio = heads // kv_heads
     assert nt == 2 and heads == n and ratio % nt == 0 and rows % BLK == 0
+    if nc == 8 and ratio == 2:
+        return halves(nc, queries, keys, values, block_lists)
     mult = nc // 2 - 1 if nc >= 4 and nc & (nc - 1) == 0 else 1
     dma, shape = pltpu.SemaphoreType.DMA, jax.ShapeDtypeStruct
     hbm = pl.BlockSpec(memory_space=pl.ANY)

time: 48.4 us -> 48.5 us (level)
  the two profiles are of different devices: /device:TPU:0 before, /device:TPU:1 now
where the time goes in v2:
time: 48.5 us; the launch traced here: 48.3 us
  Pallas kernels  46.4 us (96%)
  local copies, waits for them, and re-layouts  1.88 us (4%)
    pallas_call x1, Pallas kernels, halves(): pl.pallas_call(functools.partial(halves_kernel, nc), out_shape=jax.ShapeD...  46.4 us
    unnamed x1, local copies, waits for them, and re-layouts  1.88 us

profile of v2, /device:TPU:1, one launch (start us, length us, event | category | flops | bytes accessed | tf_op | source)
XLA Modules:
  0.0 48.3 jit_solution(17521587895009216339)
XLA Ops:
  0.0 46.4 %shard_map.46 = bf16[128,2048]{1,0:T(8,128)(2,1)} custom-call(s32[12,1,32]{2,1,0:T(1,128)} %bitcast.5, bf16[128,2048]{1,0:T(8,128)(2,1)} %q.1, bf16[2,64,1024]{2,1,0:T(8,128)(2,1)} %bitcast.3, bf16[2,64,1024]{2,1,0:T(8,128)(2,1)} %bitcast.4), custom_call_target="tpu_custom_call" | custom-call | flops 805306368 | bytes 2097152 | tf_op jit(solution)/shard_map/pallas_call | solution.py:379
  46.5 1.9 %copy.6 = bf16[128,2048]{1,0:T(8,128)(2,1)} copy(bf16[128,2048]{1,0:T(8,128)(2,1)} %shard_map.46) | data formatting | bytes 1048576

commit v3 on v1

--- a/solution.py
+++ b/solution.py
@@ -10,12 +10,13 @@
 HD = 128
 BLK = 64
 KSEL = 12
+VMEM_MIB = 60
+ORDER = (("own", 0), ("q", 0), ("up", 0), ("own", 1), ("q", 1), ("up", 1), ("own", 2), ("q", 2), ("up", 2))
 MESH = pl.DeviceIdType.MESH
 COEF = 1.4426950408889634 / (128.0**0.5)
 
 
-def attend_block(qblk, kcat, vcat, block):
-    raw = lax.dot_general(qblk, kcat, (((1,), (1,)), ((), ())), preferred_element_type=jnp.float32)
+def soften(raw, block):
     row = lax.broadcasted_iota(jnp.int32, raw.shape, 0)
     col = lax.broadcasted_iota(jnp.int32, raw.shape, 1)
     live = jnp.minimum(block + 1, KSEL) * BLK
@@ -23,9 +24,20 @@
     raw = jnp.where(keep, raw, jnp.float32(-1e30))
     top = jnp.max(raw, axis=1, keepdims=True)
     probs = jnp.exp2((raw - top) * jnp.float32(COEF))
-    total = jnp.sum(probs, axis=1, keepdims=True)
-    summed = jnp.dot(probs.astype(jnp.bfloat16), vcat, preferred_element_type=jnp.float32)
-    return (summed / total).astype(jnp.bfloat16)
+    return probs.astype(jnp.bfloat16), jnp.sum(probs, axis=1, keepdims=True)
+
+
+def attend_units(kv, units):
+    raws = []
+    for qblk, listed, _ in units:
+        kcat = jnp.concatenate([kv[0, e] for e in listed], axis=0)
+        raws.append(lax.dot_general(qblk, kcat, (((1,), (1,)), ((), ())), preferred_element_type=jnp.float32))
+    soft = [soften(raw, block) for raw, (_, _, block) in zip(raws, units)]
+    done = []
+    for (probs, total), (_, listed, _) in zip(soft, units):
+        vcat = jnp.concatenate([kv[1, e] for e in listed], axis=0)
+        done.append((jnp.dot(probs, vcat, preferred_element_type=jnp.float32) / total).astype(jnp.bfloat16))
+    return done
 
 
 def kernel(nc, nt, ratio, mult, lists, q, k, v, out, qh, kv, oh,
@@ -116,13 +128,13 @@
         score = lax.rem(t + i, nt)
         s = sc * nt + score
         drain(qh.at[part(s)], r_q.at[s])
+        units, places = [], []
         for inner in range(per):
             block = s * per + inner
-            listed = [lists[block * KSEL + slot] for slot in range(KSEL)]
-            kcat = jnp.concatenate([kv[0, i] for i in listed], axis=0)
-            vcat = jnp.concatenate([kv[1, i] for i in listed], axis=0)
-            here = pl.ds(pl.multiple_of(block * BLK, BLK), BLK)
-            oh[here, :] = attend_block(qh[here, :], kcat, vcat, block)
+            places.append(pl.ds(pl.multiple_of(block * BLK, BLK), BLK))
+            units.append((qh[places[-1], :], [lists[block * KSEL + e] for e in range(KSEL)], block))
+        for here, made in zip(places, attend_units(kv, units)):
+            oh[here, :] = made
 
         @pl.when(i == 0)
         def _():
@@ -145,6 +157,267 @@
         drain(kv.at[core, blocks(0)], s_s.at[core])
 
 
+def halves_kernel(nc, lists, q, k, v, out, lv, ls, qh, kv0, kv1, kv2, oh,
+                  s_l, r_l, c_l, s_own, s_up, s_q, s_o, s_f, s_s, l_kv, r_kv, r_f, r_s, r_q, r_o):
+    nt = 2
+    n = nc * nt
+    half = nc // 2
+    row = half // 2
+    rows = q.shape[0]
+    per = rows // BLK
+    wide = 2 * HD
+    kvs = (kv0, kv1, kv2)
+    last = len(kvs) - 1
+    c, t = lax.axis_index("seq"), lax.axis_index("tensor")
+    me = c * nt + t
+    sib = 1 - t
+    hz, cx = c // half, lax.rem(c, half)
+    base = hz * half
+    tz = cx // row
+    mine = lax.rem(cx, row) * nt + t
+    own_row = tz == t
+
+    def dev(chip, core):
+        return {"seq": chip, "tensor": core}
+
+    def key_head(p, cl):
+        return jnp.where(cl < row, 3 * cl + p, 3 * row + cl - row)
+
+    def blocks(index):
+        return pl.ds(index * per, per)
+
+    def cols(index, width):
+        return pl.ds(pl.multiple_of(index * width, width), width)
+
+    def remote(src, dst, send, recv, chip, core):
+        return pltpu.make_async_remote_copy(
+            src_ref=src, dst_ref=dst, send_sem=send, recv_sem=recv,
+            device_id=dev(chip, core), device_id_type=MESH,
+        )
+
+    def drain(ref, sem):
+        pltpu.make_async_copy(ref, ref, sem).wait()
+
+    def loop(start, stop, step):
+        def run(i, _):
+            step(i)
+            return 0
+        lax.fori_loop(start, stop, run, 0)
+
+    def where(*cases):
+        for condition, act in cases:
+            pl.when(condition)(act)
+
+    barrier = pltpu.get_barrier_semaphore()
+
+    def greet(i):
+        p = lax.rem(me + i, n)
+        pl.semaphore_signal(barrier, inc=1, device_id=dev(p // nt, lax.rem(p, nt)), device_id_type=MESH)
+
+    loop(1, n, greet)
+    pl.semaphore_wait(barrier, n - 1)
+
+    def send_kv(p, chip, sem):
+        at = cols(key_head(p, lax.rem(chip, half)), HD)
+        for core, src in ((0, k), (1, v)):
+            remote(src.at[:, :, at], kvs[p].at[core, blocks(me)], sem, r_kv.at[p, me], chip, core).start()
+
+    def dests(p):
+        return half if p == last else row
+
+    def send_up(p):
+        where((hz == 0, lambda: loop(0, dests(p), lambda i: send_kv(p, half + lax.rem(cx + i, dests(p)), s_up))))
+
+    def send_own(p):
+        def one(i):
+            cl = lax.rem(cx + i, dests(p))
+            where((cl != cx, lambda: send_kv(p, base + cl, s_own)))
+
+        loop(0, dests(p), one)
+
+        def within():
+            at = cols(key_head(p, cx), HD)
+            for core, src in ((0, k), (1, v)):
+                goal = kvs[p].at[core, blocks(me)]
+                remote(src.at[:, :, at], goal, s_s.at[p, core], r_s.at[p, core], c, sib).start()
+                pltpu.make_async_copy(src.at[:, :, at], goal, l_kv.at[p, core]).start()
+
+        where((cx < dests(p), within))
+
+    def send_q(p):
+        def one(i):
+            cl = lax.rem(cx + i, dests(p))
+            src, goal = q.at[:, cols(key_head(p, cl), wide)], qh.at[mine, p]
+            itself = (cl == cx) & own_row
+            where(
+                (itself, lambda: pltpu.make_async_copy(src, goal, r_q.at[mine, p]).start()),
+                (jnp.logical_not(itself), lambda: remote(src, goal, s_q, r_q.at[mine, p], base + cl, tz).start()),
+            )
+
+        loop(0, dests(p), one)
+
+    group = me // 2
+    early = group < 3 * row
+    list_chip = jnp.where(early, group // 3, group - 2 * row)
+    entry = jnp.where(early, lax.rem(group, 3), last) * 2 + lax.rem(me, 2)
+
+    def each_list(act_self, act_other):
+        for far in range(2):
+            for core in range(nt):
+                chip = far * half + list_chip
+                itself = (chip == c) & (t == core)
+                where(
+                    (itself, act_self),
+                    (jnp.logical_not(itself), functools.partial(act_other, far, core, chip)),
+                )
+
+    def send_lists():
+        each_list(
+            lambda: pltpu.make_async_copy(lists, lv.at[entry], r_l.at[entry]).start(),
+            lambda far, core, chip: remote(lists, lv.at[entry], s_l.at[far, core], r_l.at[entry], chip, core).start(),
+        )
+
+    send_lists()
+    for name, p in ORDER:
+        {"up": send_up, "own": send_own, "q": send_q}[name](p)
+
+    def forward(p, chip):
+        for core in range(nt):
+            here = kvs[p].at[t, blocks(chip * nt + core)]
+            drain(here, r_kv.at[p, chip * nt + core])
+            remote(here, here, s_f.at[p], r_f.at[p], c, sib).start()
+
+    def forward_own(p):
+        loop(1, half, lambda i: forward(p, base + lax.rem(cx + half - i, half)))
+
+    def forward_low(p, i):
+        where((hz == 1, lambda: forward(p, lax.rem(cx + half - i, half))))
+
+    def forward_all(p):
+        forward_own(p)
+        loop(0, half, functools.partial(forward_low, p))
+
+    def drain_forwards(p, sem):
+        where(
+            (hz == 0, lambda: drain(kvs[p].at[0, pl.ds(0, (half - 1) * nt * per)], sem)),
+            (hz == 1, lambda: drain(kvs[p].at[0, pl.ds(0, (nc - 1) * nt * per)], sem)),
+        )
+
+    def settle(p):
+        for core in range(nt):
+            drain(kvs[p].at[core, blocks(0)], r_s.at[p, core])
+            drain(kvs[p].at[core, blocks(0)], l_kv.at[p, core])
+        drain_forwards(p, r_f.at[p])
+
+    def take_lists(start, stop, sem):
+        for e in range(start, stop):
+            drain(lv.at[e], r_l.at[e])
+        some = pl.ds(start, stop - start)
+        moved = pltpu.make_async_copy(lv.at[some], ls.at[some], sem)
+        moved.start()
+        moved.wait()
+
+    def attend(p, i):
+        slot = lax.rem(mine + i, 4)
+        sc, score = base + t * row + slot // nt, lax.rem(slot, nt)
+        drain(qh.at[slot, p], r_q.at[slot, p])
+        units, places = [], []
+        for inner in range(per):
+            block = (sc * nt + score) * per + inner
+            for one in range(2):
+                listed = [ls[2 * p + one, e, 0, block] for e in range(KSEL)]
+                here = pl.ds(inner * BLK, BLK), pl.ds(one * HD, HD)
+                places.append(here)
+                units.append((qh[slot, p, here[0], here[1]], listed, block))
+        for here, made in zip(places, attend_units(kvs[p], units)):
+            oh[slot, p, here[0], here[1]] = made
+        itself = (sc == c) & (score == t)
+        head = key_head(p, cx)
+        src, goal = oh.at[slot, p], out.at[:, cols(head, wide)]
+        where(
+            (itself, lambda: pltpu.make_async_copy(src, goal, r_o.at[head]).start()),
+            (jnp.logical_not(itself), lambda: remote(src, goal, s_o, r_o.at[head], sc, score).start()),
+        )
+
+    def attend_and_forward(p, i):
+        where((i == 0, lambda: forward_own(p + 1)))
+        attend(p, i)
+        forward_low(p + 1, i)
+
+    def row_zero():
+        forward_all(0)
+        take_lists(0, 2 * last, c_l.at[0])
+        for p in range(last):
+            settle(p)
+            loop(0, 4, functools.partial(attend_and_forward, p))
+
+    where((tz == 0, row_zero), (tz == 1, lambda: forward_all(last)))
+    take_lists(2 * last, 2 * last + 2, c_l.at[1])
+    settle(last)
+    loop(0, 4, functools.partial(attend, last))
+
+    for head in range(8):
+        drain(out.at[:, pl.ds(head * wide, wide)], r_o.at[head])
+
+    def drain_q(count):
+        drain(out.at[:, pl.ds(0, count * wide)], s_q)
+
+    where(
+        (jnp.logical_not(own_row), lambda: drain_q(8)),
+        (own_row & (tz == 0), lambda: drain_q(5)),
+        (own_row & (tz == 1), lambda: drain_q(7)),
+        (jnp.logical_not(own_row) & (tz == 0), lambda: drain(oh, s_o)),
+        (jnp.logical_not(own_row) & (tz == 1), lambda: drain(oh.at[:, 0], s_o)),
+        (own_row & (tz == 0), lambda: drain(oh.at[pl.ds(0, 3)], s_o)),
+        (own_row & (tz == 1), lambda: drain(oh.at[pl.ds(0, 3), 0], s_o)),
+        (tz == 0, lambda: drain(kv0.at[0, pl.ds(0, 10 * per)], s_own)),
+        (tz == 1, lambda: drain(kv0.at[0, pl.ds(0, 14 * per)], s_own)),
+        (hz == 0, lambda: drain(kv0.at[0], s_up)),
+    )
+
+    def drain_phase(p):
+        drain_forwards(p, s_f.at[p])
+        for core in range(nt):
+            drain(kvs[p].at[core, blocks(0)], s_s.at[p, core])
+
+    where((tz == 0, lambda: [drain_phase(p) for p in range(last)] and None))
+    drain_phase(last)
+    each_list(lambda: None, lambda far, core, chip: drain(lv.at[0], s_l.at[far, core]))
+
+
+def halves(nc, queries, keys, values, block_lists):
+    rows, width = queries.shape
+    n = 2 * nc
+    per = rows // BLK
+    dma = pltpu.SemaphoreType.DMA
+    hbm = pl.BlockSpec(memory_space=pl.ANY)
+    entry = (KSEL, 1, block_lists.shape[1])
+    kv = pltpu.VMEM((2, n * per, BLK, HD), jnp.bfloat16)
+    return pl.pallas_call(
+        functools.partial(halves_kernel, nc),
+        out_shape=jax.ShapeDtypeStruct((rows, width), jnp.bfloat16),
+        in_specs=[hbm, hbm, hbm, hbm],
+        out_specs=hbm,
+        scratch_shapes=[
+            pltpu.VMEM((6, *entry), jnp.int32),
+            pltpu.SMEM((6, *entry), jnp.int32),
+            pltpu.VMEM((4, 3, rows, 2 * HD), jnp.bfloat16),
+            kv,
+            kv,
+            kv,
+            pltpu.VMEM((4, 3, rows, 2 * HD), jnp.bfloat16),
+            dma((2, 2)), dma((6,)), dma((2,)), dma, dma, dma, dma, dma((3,)), dma((3, 2)), dma((3, 2)),
+            dma((3, n)), dma((3,)), dma((3, 2)), dma((4, 3)), dma((8,)),
+        ],
+        compiler_params=pltpu.CompilerParams(
+            collective_id=0, has_side_effects=True, vmem_limit_bytes=VMEM_MIB * 2**20
+        ),
+        cost_estimate=pl.CostEstimate(
+            flops=4 * n * rows * KSEL * BLK * HD, bytes_accessed=8 * n * rows * HD, transcendentals=n * rows * KSEL * BLK
+        ),
+    )(block_lists.transpose(2, 0, 1), queries, keys.reshape(per, BLK, -1), values.reshape(per, BLK, -1))
+
+
 def body(nc, nt, queries, keys, values, block_lists):
     rows, width = queries.shape
     n = nc * nt
@@ -152,6 +425,8 @@
     kv_heads = keys.shape[1] // HD
     ratio = heads // kv_heads
     assert nt == 2 and heads == n and ratio % nt == 0 and rows % BLK == 0
+    if nc == 8 and ratio == 2:
+        return halves(nc, queries, keys, values, block_lists)
     mult = nc // 2 - 1 if nc >= 4 and nc & (nc - 1) == 0 else 1
     dma, shape = pltpu.SemaphoreType.DMA, jax.ShapeDtypeStruct
     hbm = pl.BlockSpec(memory_space=pl.ANY)

time: 48.4 us -> 42.2 us (0.87)
  the two profiles are of different devices: /device:TPU:0 before, /device:TPU:23 now
where the time goes in v3:
time: 42.2 us; the launch traced here: 41.9 us
  Pallas kernels  40 us (95%)
  local copies, waits for them, and re-layouts  1.88 us (4%)
    pallas_call x1, Pallas kernels, halves(): pl.pallas_call(functools.partial(halves_kernel, nc), out_shape=jax.ShapeD...  40 us
    unnamed x1, local copies, waits for them, and re-layouts  1.88 us

profile of v3, /device:TPU:23, one launch (start us, length us, event | category | flops | bytes accessed | tf_op | source)
XLA Modules:
  0.0 41.9 jit_solution(16473824633591399809)
XLA Ops:
  0.0 40.0 %shard_map.46 = bf16[128,2048]{1,0:T(8,128)(2,1)} custom-call(s32[12,1,32]{2,1,0:T(1,128)} %bitcast.5, bf16[128,2048]{1,0:T(8,128)(2,1)} %q.1, bf16[2,64,1024]{2,1,0:T(8,128)(2,1)} %bitcast.3, bf16[2,64,1024]{2,1,0:T(8,128)(2,1)} %bitcast.4), custom_call_target="tpu_custom_call" | custom-call | flops 805306368 | bytes 2097152 | tf_op jit(solution)/shard_map/pallas_call | solution.py:396
  40.0 1.9 %copy.6 = bf16[128,2048]{1,0:T(8,128)(2,1)} copy(bf16[128,2048]{1,0:T(8,128)(2,1)} %shard_map.46) | data formatting | bytes 1048576

commit v4 on v2

--- a/solution.py
+++ b/solution.py
@@ -15,8 +15,7 @@
 COEF = 1.4426950408889634 / (128.0**0.5)
 
 
-def attend_block(qblk, kcat, vcat, block):
-    raw = lax.dot_general(qblk, kcat, (((1,), (1,)), ((), ())), preferred_element_type=jnp.float32)
+def soften(raw, block):
     row = lax.broadcasted_iota(jnp.int32, raw.shape, 0)
     col = lax.broadcasted_iota(jnp.int32, raw.shape, 1)
     live = jnp.minimum(block + 1, KSEL) * BLK
@@ -24,9 +23,20 @@
     raw = jnp.where(keep, raw, jnp.float32(-1e30))
     top = jnp.max(raw, axis=1, keepdims=True)
     probs = jnp.exp2((raw - top) * jnp.float32(COEF))
-    total = jnp.sum(probs, axis=1, keepdims=True)
-    summed = jnp.dot(probs.astype(jnp.bfloat16), vcat, preferred_element_type=jnp.float32)
-    return (summed / total).astype(jnp.bfloat16)
+    return probs.astype(jnp.bfloat16), jnp.sum(probs, axis=1, keepdims=True)
+
+
+def attend_units(kv, units):
+    raws = []
+    for qblk, listed, _ in units:
+        kcat = jnp.concatenate([kv[0, e] for e in listed], axis=0)
+        raws.append(lax.dot_general(qblk, kcat, (((1,), (1,)), ((), ())), preferred_element_type=jnp.float32))
+    soft = [soften(raw, block) for raw, (_, _, block) in zip(raws, units)]
+    done = []
+    for (probs, total), (_, listed, _) in zip(soft, units):
+        vcat = jnp.concatenate([kv[1, e] for e in listed], axis=0)
+        done.append((jnp.dot(probs, vcat, preferred_element_type=jnp.float32) / total).astype(jnp.bfloat16))
+    return done
 
 
 def kernel(nc, nt, ratio, mult, lists, q, k, v, out, qh, kv, oh,
@@ -117,13 +127,13 @@
         score = lax.rem(t + i, nt)
         s = sc * nt + score
         drain(qh.at[part(s)], r_q.at[s])
+        units, places = [], []
         for inner in range(per):
             block = s * per + inner
-            listed = [lists[block * KSEL + slot] for slot in range(KSEL)]
-            kcat = jnp.concatenate([kv[0, i] for i in listed], axis=0)
-            vcat = jnp.concatenate([kv[1, i] for i in listed], axis=0)
-            here = pl.ds(pl.multiple_of(block * BLK, BLK), BLK)
-            oh[here, :] = attend_block(qh[here, :], kcat, vcat, block)
+            places.append(pl.ds(pl.multiple_of(block * BLK, BLK), BLK))
+            units.append((qh[places[-1], :], [lists[block * KSEL + e] for e in range(KSEL)], block))
+        for here, made in zip(places, attend_units(kv, units)):
+            oh[here, :] = made
 
         @pl.when(i == 0)
         def _():
@@ -213,8 +223,6 @@
             remote(src.at[:, :, at], kvs[j].at[core, blocks(me)], s_s.at[j, core], r_s.at[j, core], c, sib).start()
             pltpu.make_async_copy(src.at[:, :, at], kvs[j].at[core, blocks(me)], l_kv.at[j, core]).start()
 
-    send_up(0)
-
     entry = lax.rem(me, 4)
     for far in range(2):
         dc = far * half + me // 4
@@ -244,8 +252,9 @@
         send_q(0)
 
     loop(1, half, send_q)
+    send_own(1)
+    send_up(0)
     send_up(1)
-    send_own(1)
 
     def forward(j, chip):
         for core in range(nt):
@@ -286,16 +295,17 @@
         sc, score = base + t * row + slot // nt, lax.rem(slot, nt)
         if j == 0:
             drain(qh.at[slot], r_q.at[slot])
+        units, places = [], []
         for inner in range(per):
             block = (sc * nt + score) * per + inner
-            here = pl.ds(inner * BLK, BLK)
             for one in range(2):
                 head = 2 * j + one
                 listed = [ls[head, e, 0, block] for e in range(KSEL)]
-                kcat = jnp.concatenate([kvs[j][0, e] for e in listed], axis=0)
-                vcat = jnp.concatenate([kvs[j][1, e] for e in listed], axis=0)
-                qblk = qh[slot, here, pl.ds(head * HD, HD)]
-                oh[slot, j, here, pl.ds(one * HD, HD)] = attend_block(qblk, kcat, vcat, block)
+                here = pl.ds(inner * BLK, BLK)
+                places.append((here, pl.ds(one * HD, HD)))
+                units.append((qh[slot, here, pl.ds(head * HD, HD)], listed, block))
+        for here, made in zip(places, attend_units(kvs[j], units)):
+            oh[slot, j, here[0], here[1]] = made
         itself = (sc == c) & (score == t)
         goal = out.at[:, cols(cx * 2 + j, 2 * HD)]
 

time: 48.5 us -> 40.1 us (0.83)
  the two profiles are of different devices: /device:TPU:1 before, /device:TPU:23 now
where the time goes in v4:
time: 40.1 us; the launch traced here: 39.6 us
  Pallas kernels  37.7 us (94%)
  local copies, waits for them, and re-layouts  1.88 us (5%)
    pallas_call x1, Pallas kernels, halves(): pl.pallas_call(functools.partial(halves_kernel, nc), out_shape=jax.ShapeD...  37.7 us
    unnamed x1, local copies, waits for them, and re-layouts  1.88 us

profile of v4, /device:TPU:23, one launch (start us, length us, event | category | flops | bytes accessed | tf_op | source)
XLA Modules:
  0.0 39.6 jit_solution(1172534741606126555)
XLA Ops:
  0.0 37.7 %shard_map.46 = bf16[128,2048]{1,0:T(8,128)(2,1)} custom-call(s32[12,1,32]{2,1,0:T(1,128)} %bitcast.5, bf16[128,2048]{1,0:T(8,128)(2,1)} %q.1, bf16[2,64,1024]{2,1,0:T(8,128)(2,1)} %bitcast.3, bf16[2,64,1024]{2,1,0:T(8,128)(2,1)} %bitcast.4), custom_call_target="tpu_custom_call" | custom-call | flops 805306368 | bytes 2097152 | tf_op jit(solution)/shard_map/pallas_call | solution.py:389
  37.7 1.9 %copy.6 = bf16[128,2048]{1,0:T(8,128)(2,1)} copy(bf16[128,2048]{1,0:T(8,128)(2,1)} %shard_map.46) | data formatting | bytes 1048576

commit v5 on v4

--- a/solution.py
+++ b/solution.py
@@ -388,7 +388,7 @@
     kv = pltpu.VMEM((2, n * per, BLK, HD), jnp.bfloat16)
     return pl.pallas_call(
         functools.partial(halves_kernel, nc),
-        out_shape=jax.ShapeDtypeStruct((rows, width), jnp.bfloat16),
+        out_shape=pltpu.VMEM((rows, width), jnp.bfloat16),
         in_specs=[hbm, hbm, hbm, hbm],
         out_specs=hbm,
         scratch_shapes=[

time: 40.1 us -> 38.9 us (0.970)
  local copies, waits for them, and re-layouts: 1.88 us -> 0.8 us
    unnamed x1, local copies, waits for them, and re-layouts: 1.88 us -> 0.8 us
where the time goes in v5:
time: 38.9 us; the launch traced here: 38.4 us
  Pallas kernels  37.6 us (97%)
  local copies, waits for them, and re-layouts  0.8 us (2%)
    pallas_call x1, Pallas kernels, halves(): pl.pallas_call(functools.partial(halves_kernel, nc), out_shape=pltpu.VMEM...  37.6 us
    unnamed x1, local copies, waits for them, and re-layouts  0.8 us

profile of v5, /device:TPU:23, one launch (start us, length us, event | category | flops | bytes accessed | tf_op | source)
XLA Modules:
  0.0 38.4 jit_solution(14173566269635983419)
XLA Ops:
  0.0 37.6 %shard_map.46 = bf16[128,2048]{1,0:T(8,128)(2,1)S(1)} custom-call(s32[12,1,32]{2,1,0:T(1,128)} %bitcast.5, bf16[128,2048]{1,0:T(8,128)(2,1)} %q.1, bf16[2,64,1024]{2,1,0:T(8,128)(2,1)} %bitcast.3, bf16[2,64,1024]{2,1,0:T(8,128)(2,1)} %bitcast.4), custom_call_target="tpu_custom_call" | custom-call | flops 805306368 | bytes 2097152 | tf_op jit(solution)/shard_map/pallas_call | solution.py:389
  37.6 0.8 %copy.6 = bf16[128,2048]{1,0:T(8,128)(2,1)} copy(bf16[128,2048]{1,0:T(8,128)(2,1)S(1)} %shard_map.46) | data formatting | bytes 1048576

commit v6 on v5

--- a/solution.py
+++ b/solution.py
@@ -291,7 +291,7 @@
     pltpu.make_async_copy(lv, ls, c_l).wait()
 
     def attend(j, i):
-        slot = lax.rem(mine + i, 4)
+        slot = lax.rem(mine // nt + 1 + i // nt, 2) * nt + lax.rem(t + 1 + i, nt)
         sc, score = base + t * row + slot // nt, lax.rem(slot, nt)
         if j == 0:
             drain(qh.at[slot], r_q.at[slot])

time: 38.9 us -> 38 us (0.977)
  Pallas kernels: 37.6 us -> 36.6 us
    pallas_call x1, Pallas kernels: 37.6 us -> 36.6 us  [halves(): pl.pallas_call(functools.partial(halves_kernel, nc), out_shape=pltpu.VMEM...]
where the time goes in v6:
time: 38 us; the launch traced here: 37.4 us
  Pallas kernels  36.6 us (96%)
  local copies, waits for them, and re-layouts  0.8 us (2%)
    pallas_call x1, Pallas kernels, halves(): pl.pallas_call(functools.partial(halves_kernel, nc), out_shape=pltpu.VMEM...  36.6 us
    unnamed x1, local copies, waits for them, and re-layouts  0.8 us

profile of v6, /device:TPU:23, one launch (start us, length us, event | category | flops | bytes accessed | tf_op | source)
XLA Modules:
  0.0 37.4 jit_solution(12518506005668417243)
XLA Ops:
  0.0 36.6 %shard_map.46 = bf16[128,2048]{1,0:T(8,128)(2,1)S(1)} custom-call(s32[12,1,32]{2,1,0:T(1,128)} %bitcast.5, bf16[128,2048]{1,0:T(8,128)(2,1)} %q.1, bf16[2,64,1024]{2,1,0:T(8,128)(2,1)} %bitcast.3, bf16[2,64,1024]{2,1,0:T(8,128)(2,1)} %bitcast.4), custom_call_target="tpu_custom_call" | custom-call | flops 805306368 | bytes 2097152 | tf_op jit(solution)/shard_map/pallas_call | solution.py:389
  36.6 0.8 %copy.6 = bf16[128,2048]{1,0:T(8,128)(2,1)} copy(bf16[128,2048]{1,0:T(8,128)(2,1)S(1)} %shard_map.46) | data formatting | bytes 1048576

commit v7 on v6

--- a/solution.py
+++ b/solution.py
@@ -16,11 +16,15 @@
 
 
 def soften(raw, block):
-    row = lax.broadcasted_iota(jnp.int32, raw.shape, 0)
-    col = lax.broadcasted_iota(jnp.int32, raw.shape, 1)
     live = jnp.minimum(block + 1, KSEL) * BLK
+    first, rest = raw[:, : 2 * BLK], raw[:, 2 * BLK :]
+    row = lax.broadcasted_iota(jnp.int32, first.shape, 0)
+    col = lax.broadcasted_iota(jnp.int32, first.shape, 1)
     keep = ((col >= BLK) | (col <= row)) & (col < live)
-    raw = jnp.where(keep, raw, jnp.float32(-1e30))
+    later = lax.broadcasted_iota(jnp.int32, rest.shape, 1) < live - 2 * BLK
+    first = jnp.where(keep, first, jnp.float32(-1e30))
+    rest = jnp.where(later, rest, jnp.float32(-1e30))
+    raw = jnp.concatenate([first, rest], axis=1)
     top = jnp.max(raw, axis=1, keepdims=True)
     probs = jnp.exp2((raw - top) * jnp.float32(COEF))
     return probs.astype(jnp.bfloat16), jnp.sum(probs, axis=1, keepdims=True)

time: 38 us -> 38 us (level)
  no operation moved by 1% of the time
where the time goes in v7:
time: 38 us; the launch traced here: 37.4 us
  Pallas kernels  36.6 us (96%)
  local copies, waits for them, and re-layouts  0.8 us (2%)
    pallas_call x1, Pallas kernels, halves(): pl.pallas_call(functools.partial(halves_kernel, nc), out_shape=pltpu.VMEM...  36.6 us
    unnamed x1, local copies, waits for them, and re-layouts  0.8 us

profile of v7, /device:TPU:23, one launch (start us, length us, event | category | flops | bytes accessed | tf_op | source)
XLA Modules:
  0.0 37.4 jit_solution(16031465834166358818)
XLA Ops:
  0.0 36.6 %shard_map.46 = bf16[128,2048]{1,0:T(8,128)(2,1)S(1)} custom-call(s32[12,1,32]{2,1,0:T(1,128)} %bitcast.5, bf16[128,2048]{1,0:T(8,128)(2,1)} %q.1, bf16[2,64,1024]{2,1,0:T(8,128)(2,1)} %bitcast.3, bf16[2,64,1024]{2,1,0:T(8,128)(2,1)} %bitcast.4), custom_call_target="tpu_custom_call" | custom-call | flops 805306368 | bytes 2097152 | tf_op jit(solution)/shard_map/pallas_call | solution.py:393
  36.6 0.8 %copy.6 = bf16[128,2048]{1,0:T(8,128)(2,1)} copy(bf16[128,2048]{1,0:T(8,128)(2,1)S(1)} %shard_map.46) | data formatting | bytes 1048576

commit v8 on v6

--- a/solution.py
+++ b/solution.py
@@ -291,7 +291,7 @@
     pltpu.make_async_copy(lv, ls, c_l).wait()
 
     def attend(j, i):
-        slot = lax.rem(mine // nt + 1 + i // nt, 2) * nt + lax.rem(t + 1 + i, nt)
+        slot = lax.rem(mine // nt + 1 + i // nt, 2) * nt + lax.rem(t + i, nt)
         sc, score = base + t * row + slot // nt, lax.rem(slot, nt)
         if j == 0:
             drain(qh.at[slot], r_q.at[slot])

time: 38 us -> 38 us (level); the launches traced: 37.4 us -> 37.8 us
  Pallas kernels: 36.6 us -> 37 us
    pallas_call x1, Pallas kernels: 36.6 us -> 37 us  [halves(): pl.pallas_call(functools.partial(halves_kernel, nc), out_shape=pltpu.VMEM...]
where the time goes in v8:
time: 38 us; the launch traced here: 37.8 us
  Pallas kernels  37 us (97%)
  local copies, waits for them, and re-layouts  0.8 us (2%)
    pallas_call x1, Pallas kernels, halves(): pl.pallas_call(functools.partial(halves_kernel, nc), out_shape=pltpu.VMEM...  37 us
    unnamed x1, local copies, waits for them, and re-layouts  0.8 us

profile of v8, /device:TPU:23, one launch (start us, length us, event | category | flops | bytes accessed | tf_op | source)
XLA Modules:
  0.0 37.8 jit_solution(15565379645567648850)
XLA Ops:
  0.0 37.0 %shard_map.46 = bf16[128,2048]{1,0:T(8,128)(2,1)S(1)} custom-call(s32[12,1,32]{2,1,0:T(1,128)} %bitcast.5, bf16[128,2048]{1,0:T(8,128)(2,1)} %q.1, bf16[2,64,1024]{2,1,0:T(8,128)(2,1)} %bitcast.3, bf16[2,64,1024]{2,1,0:T(8,128)(2,1)} %bitcast.4), custom_call_target="tpu_custom_call" | custom-call | flops 805306368 | bytes 2097152 | tf_op jit(solution)/shard_map/pallas_call | solution.py:389
  37.0 0.8 %copy.6 = bf16[128,2048]{1,0:T(8,128)(2,1)} copy(bf16[128,2048]{1,0:T(8,128)(2,1)S(1)} %shard_map.46) | data formatting | bytes 1048576
